TPU v7x, 1024 devices: a whole 4x4x32 slice. The times are simulated.
1024 devices in a mesh: space: 32 (over y, x, core), freq: 32 (over z).
Axes of the slice: x: 4, y: 4, z: 32, core: 2. Of those that a mesh axis runs over, the one named last changes fastest.
Arguments:
- snapshots: bfloat16 [131072, 8192], P('space', 'freq'), may hold values from -6 to 6
- tail: bfloat16 [131072, 128], P('space'), may hold values from -6 to 6
Outputs:
- gram: float32 [128, 2, 64, 64], P('freq', None, 'space')
- spectrum: float32 [128], P('freq')
All inputs are finite; a program needn't handle non-finite values.
Results may differ from a plain program's by a relative error of at most 0.0038.
Values may be sent and summed in bfloat16 or wider, within the bound.
No kernel may reach another device: no remote copies, remote signals or barrier semaphores. Data moves between devices by JAX's collectives and lax.ppermute only.
A program may use at most 64 MiB of HBM per device.

v0:
```python
import math

import jax
import jax.numpy as jnp
from jax import lax
from jax.sharding import PartitionSpec as P

FREQ_DEV = 4
NFFT = 256
POWER = 4


def shifted(value, axis, steps):
    count = lax.axis_size(axis)
    initial, last = (max(0, -steps), min(count, count - steps))
    return lax.ppermute(value, axis, [(source, source + steps) for source in range(initial, last)])


def build_table(count):
    steps = jnp.arange(NFFT, dtype=jnp.int32)
    freqs = jnp.arange(count, dtype=jnp.int32)
    window = 0.5 - 0.5 * jnp.cos(2.0 * math.pi * steps.astype(jnp.float32) / NFFT)
    phase = 2.0 * math.pi * (steps[:, None] * freqs[None, :] % NFFT).astype(jnp.float32) / NFFT
    table = jnp.concatenate(
        [window[:, None] * jnp.cos(phase), -window[:, None] * jnp.sin(phase)], 1
    )
    return (table.astype(jnp.bfloat16), jnp.sum(window * window))


def transform(extended, table):
    points, width = extended.shape
    half = NFFT // 2
    count = width // half - 1
    halves = extended.reshape(points, count + 1, half)
    blocks = jnp.concatenate([halves[:, :-1], halves[:, 1:]], 2)
    coef = jnp.einsum("pbt,tk->bkp", blocks, table, preferred_element_type=jnp.float32)
    return coef.reshape(count, 2, table.shape[1] // 2, points).astype(jnp.bfloat16)


def gram_terms(coef, scale):
    big = jnp.einsum("bcfp,gdfp->fcbdg", coef, coef, preferred_element_type=jnp.float32)
    real = big[:, 0, :, 0, :] + big[:, 1, :, 1, :]
    imag = big[:, 0, :, 1, :] - big[:, 1, :, 0, :]
    return jnp.stack([real, imag], 1) * scale


def apply_matrix(matrix, vector):
    high = lax.Precision.HIGHEST
    m_real, m_imag = (matrix[:, 0], matrix[:, 1])
    v_real, v_imag = (vector[:, 0], vector[:, 1])
    u_real = jnp.einsum("fjk,fk->fj", m_real, v_real, precision=high) - jnp.einsum(
        "fjk,fk->fj", m_imag, v_imag, precision=high
    )
    u_imag = jnp.einsum("fjk,fk->fj", m_real, v_imag, precision=high) + jnp.einsum(
        "fjk,fk->fj", m_imag, v_real, precision=high
    )
    return jnp.stack([u_real, u_imag], 1)


def rescale(product):
    return product / jnp.sqrt(jnp.mean(product * product, axis=(1, 2), keepdims=True) + 1e-06)


def rayleigh(vector, product):
    return jnp.mean(vector * product, axis=(1, 2)) / (
        jnp.mean(vector * vector, axis=(1, 2)) + 1e-06
    )


def shards(snapshots, tail):
    points = snapshots.shape[0]
    freq_count = lax.axis_size("freq")
    half = NFFT // 2
    table, wsum = build_table(FREQ_DEV * freq_count)
    scale = 1.0 / (points * lax.axis_size("space") * wsum)
    following = shifted(snapshots[:, :half], "freq", -1)
    is_last = lax.axis_index("freq") == freq_count - 1
    following = jnp.where(is_last, tail, following)
    extended = jnp.concatenate([snapshots, following], 1)
    coef = transform(extended, table)
    regrouped = lax.all_to_all(coef, "freq", split_axis=2, concat_axis=0, tiled=True)
    partial_value = gram_terms(regrouped, scale)
    blocks_all = partial_value.shape[2]
    held = blocks_all // lax.axis_size("space")
    vector = jnp.stack(
        [
            jnp.ones((FREQ_DEV, blocks_all), jnp.float32),
            jnp.zeros((FREQ_DEV, blocks_all), jnp.float32),
        ],
        1,
    )
    total = lax.psum(partial_value, "space")
    for step in range(POWER):
        vector = rescale(apply_matrix(total, vector))
    spectrum = rayleigh(vector, apply_matrix(total, vector))
    gram_rows = lax.dynamic_slice_in_dim(total, lax.axis_index("space") * held, held, 2)
    return (gram_rows, spectrum)


def solution(mesh):
    in_specs = (P("space", "freq"), P("space", None))
    out_specs = (P("freq", None, "space", None), P("freq"))
    return jax.shard_map(shards, mesh=mesh, in_specs=in_specs, out_specs=out_specs, check_vma=False)
```

profile of v0, /device:TPU:1, one launch (start us, length us, event | category | flops | bytes accessed | tf_op | source)
XLA Modules:
  0.0 678.2 jit_solution(1191759778161750787)
XLA Ops:
  7.2 2.9 copy.29
  10.1 1.1 slice.76
  11.2 1.3 collective-permute-start
  12.4 1.5 copy.28
  14.0 0.5 multiply_convert_fusion
  14.6 13.4 %collective-permute-done = bf16[4096,128]{0,1:T(8,128)(2,1)} collective-permute-done((bf16[4096,128]{0,1:T(8,128)(2,1)}, bf16[4096,128]{0,1:T(8,128)(2,1)}, u32[]{:S(2)}, u32[]{:S(2)}) %collective-permute-start) | collective-permute-done | bytes 1048608 | tf_op jit(solution)/shard_map/ppermute | solution.py:16
  28.0 1.3 broadcast_select_fusion
  29.4 0.2 pad_maximum_fusion
  29.6 1.8 fusion.49
  31.4 4.1 copy.69
  35.5 2.5 copy.70
  38.0 3.5 convolution_convert_fusion
  41.5 6.3 copy.32
  47.8 38.8 %all-to-all-start = ((bf16[2,2,128,4096]{3,1,0,2:T(2,128)(2,1)}), bf16[2,2,128,4096]{3,1,0,2:T(2,128)(2,1)}, u32[]{:S(2)}, u32[]{:S(2)}) async-start(bf16[2,2,128,4096]{3,1,0,2:T(2,128)(2,1)} %copy.32), calls=%async_computation | async-start | bytes 8388608 | tf_op jit(solution)/shard_map/all_to_all | solution.py:81
  86.6 0.2 all-reduce.2.cloned.1.call-start
  86.8 0.6 multiply_reduce_fusion.5
  88.2 359.8 %all-to-all-done = bf16[2,2,128,4096]{3,1,0,2:T(2,128)(2,1)} async-done(((bf16[2,2,128,4096]{3,1,0,2:T(2,128)(2,1)}), bf16[2,2,128,4096]{3,1,0,2:T(2,128)(2,1)}, u32[]{:S(2)}, u32[]{:S(2)}) %all-to-all-start) | async-done | bytes 4194336 | tf_op jit(solution)/shard_map/all_to_all | solution.py:81
  448.0 9.7 %copy.74 = bf16[2,2,32,4,4096]{4,0,2,1,3:T(2,128)(2,1)} copy(bf16[2,2,32,4,4096]{4,1,0,3,2:T(2,128)(2,1)} %bitcast.4) | data formatting | bytes 8388608 | tf_op jit(solution)/shard_map/all_to_all | solution.py:81
  457.6 7.2 %reshape.91 = bf16[64,2,4,4096,1]{3,0,1,2,4:T(8,128)(2,1)} reshape(bf16[32,2,2,4,4096]{4,1,0,2,3:T(2,128)(2,1)} %bitcast.178) | data formatting | bytes 8388608 | tf_op jit(solution)/shard_map/all_to_all | solution.py:81
  464.9 5.8 fusion.6
  470.7 0.7 maximum_multiply_fusion
  471.4 173.7 %all-reduce.2.cloned.1.call-done = f32[4,2,64,64]{2,3,0,1:T(8,128)} async-done(((f32[4,2,64,64]{2,3,0,1:T(8,128)}), f32[4,2,64,64]{2,3,0,1:T(8,128)}) %all-reduce.2.cloned.1.call-update) | async-done | bytes 131088 | tf_op jit(solution)/shard_map/psum | solution.py:92
  645.1 1.1 fusion.31
  646.3 1.1 fusion.41
  647.4 1.1 fusion.30
  648.5 1.1 fusion.40
  649.7 0.1 multiply_reduce_fusion.4
  649.9 1.1 fusion.39
  651.0 1.1 fusion.29
  652.2 1.1 fusion.38
  653.3 1.1 fusion.28
  654.4 0.1 multiply_reduce_fusion.3
  654.7 1.1 fusion.37
  655.8 1.1 fusion.27
  656.9 1.1 fusion.36
  658.1 1.1 fusion.26
  659.4 1.1 fusion.35
  660.6 1.1 fusion.25
  661.7 1.1 fusion.34
  662.8 1.1 fusion.24
  664.2 1.1 constant_dynamic-slice_fusion
  665.3 0.7 copy.36
  666.0 1.1 fusion.33
  667.2 1.1 fusion.23
  668.3 1.1 fusion.32
  669.4 1.1 fusion.22
  670.6 0.2 fusion.42
  670.8 0.5 add_divide_fusion
  (31 shorter events, 0.8 us)
Async XLA Ops:
  11.2 16.9 %collective-permute-start = (bf16[4096,128]{0,1:T(8,128)(2,1)}, bf16[4096,128]{0,1:T(8,128)(2,1)}, u32[]{:S(2)}, u32[]{:S(2)}) collective-permute-start(bf16[4096,128]{0,1:T(8,128)(2,1)} %slice.76), channel_id=1, source_target_pairs={{1,0},{2,1},{3,2},{4,3},{5,4},{6,5},{7,6},{8,7},{9,8},{10,9},{11,1... | collective-permute-start | bytes 3145736 | tf_op jit(solution)/shard_map/ppermute | solution.py:16
  47.8 400.1 %all-to-all-start = ((bf16[2,2,128,4096]{3,1,0,2:T(2,128)(2,1)}), bf16[2,2,128,4096]{3,1,0,2:T(2,128)(2,1)}, u32[]{:S(2)}, u32[]{:S(2)}) async-start(bf16[2,2,128,4096]{3,1,0,2:T(2,128)(2,1)} %copy.32), calls=%async_computation | async-start | bytes 8388608 | tf_op jit(solution)/shard_map/all_to_all | solution.py:81
  86.6 558.5 %all-reduce.2.cloned.1.call-start = ((), (), s32[]{:S(2)}) async-start(), calls=%async_computation.1 | async-start | bytes 524288 | tf_op jit(solution)/shard_map/psum | solution.py:92
Sparse Core Ops, SparseCore 0:
  471.6 173.5 all-reduce.1
where the time goes:
time: 679 us; the launch traced here: 678 us
  waiting for transfers between devices  547 us (81%)
  starting transfers between devices  40.3 us (6%)
  local copies, waits for them, and re-layouts  38.9 us (6%)
  matrix products  31.9 us (5%)
  between operations  14.9 us (2%)
    all_to_all x1, waiting for transfers between devices, shards(): lax.all_to_all(coef, 'freq', split_axis=2, concat_axis=0, tiled=True)  360 us
    psum x1, waiting for transfers between devices, shards(): total = lax.psum(partial_value, 'space')  174 us
    all_to_all x1, starting transfers between devices, shards(): lax.all_to_all(coef, 'freq', split_axis=2, concat_axis=0, tiled=True)  38.8 us
    all_to_all x2, local copies, waits for them, and re-layouts, shards(): lax.all_to_all(coef, 'freq', split_axis=2, concat_axis=0, tiled=True)  16.9 us
  transfers between devices with their start and end apart: 3, of which 3 were waited for; matrix products, arithmetic and copies ran while one was open for 0% of the time, Pallas kernels for 0%

commit v1 on v0

v1 whole, which is shorter than its diff:
```python
import math

import jax
import jax.numpy as jnp
import numpy as np
from jax import lax
from jax.experimental import pallas as pl
from jax.experimental.pallas import tpu as pltpu
from jax.sharding import PartitionSpec as P

NFFT = 256
HALF = NFFT // 2
POWER = 4
BLOCKS = 64
FREQS = 128
PITCH = 2 * FREQS + 8
GROUPS = 32
NT = (((1,), (1,)), ((), ()))


def build_table():
    steps = jnp.arange(NFFT, dtype=jnp.int32)
    freqs = jnp.arange(FREQS, dtype=jnp.int32)
    window = 0.5 - 0.5 * jnp.cos(2.0 * math.pi * steps.astype(jnp.float32) / NFFT)
    phase = 2.0 * math.pi * (freqs[:, None] * steps[None, :] % NFFT).astype(jnp.float32) / NFFT
    table = jnp.concatenate(
        [window[None, :] * jnp.cos(phase), -window[None, :] * jnp.sin(phase)], 0
    )
    return (table.astype(jnp.bfloat16), jnp.sum(window * window))


def gram_kernel(factor_ref, raw_ref, tail_ref, table_ref, out_ref, coef_ref, sums_ref):
    points = raw_ref.shape[1]

    def put(block, rows):
        coef = lax.dot_general(table_ref[...], rows, NT, preferred_element_type=jnp.float32)
        start = pl.multiple_of(block * PITCH, 8)
        coef_ref[pl.ds(start, 2 * FREQS), :] = coef

    def transform(z, carry):
        rows = raw_ref[z]
        put(2 * z, rows)
        put(2 * z + 1, jnp.concatenate([rows[:, HALF:], raw_ref[z + 1][:, :HALF]], 1))
        return carry

    lax.fori_loop(0, GROUPS - 1, transform, 0, unroll=True)
    rows = raw_ref[GROUPS - 1]
    put(2 * GROUPS - 2, rows)
    put(2 * GROUPS - 1, jnp.concatenate([rows[:, HALF:], tail_ref[...]], 1))

    row = lax.broadcasted_iota(jnp.int32, (BLOCKS, 2 * BLOCKS), 0)
    lane = lax.broadcasted_iota(jnp.int32, (BLOCKS, 2 * BLOCKS), 1)
    first = ((lane < BLOCKS) & (row <= lane)) | ((lane >= BLOCKS) & (row > lane - BLOCKS))

    def product(f, swap):
        real = coef_ref[pl.ds(f, BLOCKS, stride=PITCH), :].astype(jnp.bfloat16)
        imag = coef_ref[pl.ds(FREQS + f, BLOCKS, stride=PITCH), :].astype(jnp.bfloat16)
        left = jnp.concatenate([real, imag], 1)
        turned = jnp.concatenate([imag, -real], 1)
        right = jnp.concatenate([turned, left] if swap else [left, turned], 0)
        return lax.dot_general(left, right, NT, preferred_element_type=jnp.float32)

    def packed(f):
        return jnp.where(first, product(f, False), product(f + 1, True))

    def gram(step, carry):
        base = 8 * step
        for core in range(2):
            upper = packed(base + 2 * core)
            lower = packed(base + 4 + 2 * core)
            for chip in range(GROUPS // 2):
                part = slice(4 * chip, 4 * chip + 4)
                start = pl.multiple_of(base, 8)
                sums_ref[2 * chip + core, pl.ds(start, 8), :] = jnp.concatenate(
                    [upper[part], lower[part]], 0
                )
        return carry

    lax.fori_loop(0, FREQS // 8, gram, 0, unroll=2)
    factor = factor_ref[0]
    for index in range(GROUPS):
        out_ref[index] = (sums_ref[index] * factor).astype(jnp.bfloat16)


def gram_call(factor, raw, tail, table):
    points = raw.shape[1]
    return pl.pallas_call(
        gram_kernel,
        out_shape=jax.ShapeDtypeStruct((GROUPS, FREQS, 2 * BLOCKS), jnp.bfloat16),
        in_specs=[
            pl.BlockSpec(memory_space=pltpu.SMEM),
            pl.BlockSpec(memory_space=pltpu.VMEM),
            pl.BlockSpec(memory_space=pltpu.VMEM),
            pl.BlockSpec(memory_space=pltpu.VMEM),
        ],
        out_specs=pl.BlockSpec(memory_space=pltpu.VMEM),
        scratch_shapes=[
            pltpu.VMEM((BLOCKS * PITCH, points), jnp.float32),
            pltpu.VMEM((GROUPS, FREQS, 2 * BLOCKS), jnp.float32),
        ],
        compiler_params=pltpu.CompilerParams(vmem_limit_bytes=40 * 1024 * 1024),
        name="gram",
    )(factor, raw, tail, table)


def power_kernel(place_ref, scale_ref, sums_ref, rows_ref, spectrum_ref, matrix_ref):
    scale = scale_ref[0]
    row = lax.broadcasted_iota(jnp.int32, (BLOCKS, BLOCKS), 0)
    column = lax.broadcasted_iota(jnp.int32, (BLOCKS, BLOCKS), 1)
    matrices = []
    for core in range(2):
        held = jnp.concatenate([sums_ref[2 * c + core] for c in range(GROUPS // 2)], 0) * scale
        left, right = (held[:, :BLOCKS], held[:, BLOCKS:])
        left_t, right_t = (left.T, right.T)
        real_even = jnp.where(row <= column, left, left_t)
        real_odd = jnp.where(row <= column, right, right_t)
        zero = jnp.zeros_like(left)
        imag_odd = jnp.where(row > column, left, jnp.where(row < column, -left_t, zero))
        imag_even = jnp.where(row > column, right, jnp.where(row < column, -right_t, zero))
        matrices.append(jnp.concatenate([real_even, imag_even], 1))
        matrices.append(jnp.concatenate([real_odd, imag_odd], 1))
    matrix = jnp.stack(matrices, 0)
    matrix_ref[...] = matrix
    place = place_ref[0]
    for k in range(2):
        rows_ref[:, k : k + 1, :] = matrix_ref[:, pl.ds(2 * place + k, 1), :]

    low = lax.broadcasted_iota(jnp.int32, (4, 1, 2 * BLOCKS), 2) < BLOCKS
    count = 2.0 * BLOCKS

    def turn(v):
        return jnp.concatenate([v[:, :, BLOCKS:], v[:, :, :BLOCKS]], 2)

    def from_columns(v_real, v_imag):
        a = jnp.sum(matrix * v_real, axis=1, keepdims=True)
        b = jnp.sum(matrix * v_imag, axis=1, keepdims=True)
        return jnp.where(low, a, -a) + turn(b)

    def from_rows(v):
        u_real = jnp.sum(matrix * jnp.where(low, v, -v), axis=2, keepdims=True)
        u_imag = jnp.sum(matrix * turn(v), axis=2, keepdims=True)
        return (u_real, u_imag)

    def scaled_columns(u_real, u_imag):
        m = jnp.sum(u_real * u_real + u_imag * u_imag, axis=1, keepdims=True) / count
        norm = jnp.sqrt(m + 1e-06)
        return (u_real / norm, u_imag / norm)

    def scaled_rows(u):
        return u / jnp.sqrt(jnp.sum(u * u, axis=2, keepdims=True) / count + 1e-06)

    v = jnp.where(low, jnp.ones((4, 1, 2 * BLOCKS), jnp.float32), 0.0)
    for step in range(POWER // 2):
        v = scaled_rows(from_columns(*scaled_columns(*from_rows(v))))
    u_real, u_imag = from_rows(v)
    lane = lax.broadcasted_iota(jnp.int32, (4, BLOCKS, 2 * BLOCKS), 2)
    line = lax.broadcasted_iota(jnp.int32, (4, BLOCKS, 2 * BLOCKS), 1)
    v_real = jnp.sum(jnp.where(lane == line, v, 0.0), axis=2, keepdims=True)
    v_imag = jnp.sum(jnp.where(lane == line + BLOCKS, v, 0.0), axis=2, keepdims=True)
    top = jnp.sum(v_real * u_real + v_imag * u_imag, axis=1, keepdims=True) / count
    below = jnp.sum(v_real * v_real + v_imag * v_imag, axis=1, keepdims=True) / count
    spectrum_ref[...] = jnp.broadcast_to(top / (below + 1e-06), spectrum_ref.shape)


def power_call(place, scale, sums):
    return pl.pallas_call(
        power_kernel,
        out_shape=(
            jax.ShapeDtypeStruct((4, 2, 2 * BLOCKS), jnp.float32),
            jax.ShapeDtypeStruct((4, 1, 2 * BLOCKS), jnp.float32),
        ),
        in_specs=[
            pl.BlockSpec(memory_space=pltpu.SMEM),
            pl.BlockSpec(memory_space=pltpu.SMEM),
            pl.BlockSpec(memory_space=pltpu.VMEM),
        ],
        out_specs=(
            pl.BlockSpec(memory_space=pltpu.VMEM),
            pl.BlockSpec(memory_space=pltpu.VMEM),
        ),
        scratch_shapes=[pltpu.VMEM((4, BLOCKS, 2 * BLOCKS), jnp.float32)],
        compiler_params=pltpu.CompilerParams(vmem_limit_bytes=16 * 1024 * 1024),
        name="power",
    )(place, scale, sums)


def shards(snapshots, tail):
    points = snapshots.shape[0]
    space = lax.axis_index("space")
    freq = lax.axis_index("freq")
    each = points // GROUPS
    table, wsum = build_table()
    scale = 1.0 / (points * GROUPS * wsum)
    raw = lax.all_to_all(snapshots.reshape(GROUPS, each, NFFT), "freq", 0, 0)
    own_tail = lax.dynamic_slice_in_dim(tail, freq * each, each, 0)
    factors = np.exp2(np.arange(GROUPS) / GROUPS).astype(np.float32)
    factor = jnp.exp2(space.astype(jnp.float32) / GROUPS)
    sums = gram_call(factor.reshape(1), raw, own_tail, table)
    parts = lax.all_to_all(sums, "space", 0, 0)
    undo = jnp.asarray(1.0 / factors, jnp.float32)[:, None, None]
    mine = jnp.sum(parts.astype(jnp.float32) * undo, 0).reshape(GROUPS, 4, 2 * BLOCKS)
    mine = jnp.sum(lax.all_to_all(mine, "freq", 0, 0), 0)
    whole = lax.all_to_all(jnp.broadcast_to(mine[None], (GROUPS,) + mine.shape), "space", 0, 0)
    rows, spectrum = power_call(space.reshape(1), scale.reshape(1), whole)
    return (rows.reshape(4, 2, 2, BLOCKS).transpose(0, 2, 1, 3), spectrum[:, 0, 0])


def solution(mesh):
    in_specs = (P("space", "freq"), P("space", None))
    out_specs = (P("freq", None, "space", None), P("freq"))
    return jax.shard_map(shards, mesh=mesh, in_specs=in_specs, out_specs=out_specs, check_vma=False)
```

time: 679 us -> 305 us (0.45)
  waiting for transfers between devices: 547 us -> 198 us
  blocking collectives: 0 us -> 59.1 us
  local copies, waits for them, and re-layouts: 38.9 us -> 1.98 us
  matrix products: 31.9 us -> 0 us
  between operations: 14.9 us -> 1.44 us
  Pallas kernels: 0 us -> 7.66 us
    psum x1 -> x0, waiting for transfers between devices: 174 us -> none  [shards(): total = lax.psum(partial_value, 'space')]
    all_to_all x1 -> x2, waiting for transfers between devices: 360 us -> 198 us  [the longest x1 192 us: shards(): raw = lax.all_to_all(snapshots.reshape(GROUPS, each, NFFT), 'freq', 0, 0)]
    all_to_all x0 -> x2, blocking collectives: none -> 59.1 us  [the longest x1 34.5 us: shards(): mine = jnp.sum(lax.all_to_all(mine, 'freq', 0, 0), 0)]
    dot_general x22 -> x0, matrix products: 31.9 us -> none  [the longest x1 5.78 us: gram_terms(): jnp.einsum('bcfp,gdfp->fcbdg', coef, coef, preferred_element_type=jnp.flo...]
    all_to_all x2 -> x0, local copies, waits for them, and re-layouts: 16.9 us -> none  [shards(): lax.all_to_all(coef, 'freq', split_axis=2, concat_axis=0, tiled=True)]
    ppermute x1 -> x0, waiting for transfers between devices: 13.4 us -> none  [shifted(): lax.ppermute(value, axis, [(source, source + steps) for source in range(i...]
    unnamed x5 -> x4, local copies, waits for them, and re-layouts: 11.7 us -> 0.01 us
    pallas_call x0 -> x2, Pallas kernels: none -> 7.66 us  [the longest x1 6.37 us: gram_call(): pl.pallas_call(gram_kernel, out_shape=jax.ShapeDtypeStruct((GROUPS, FREQS...]
  transfers between devices with their start and end apart: 3 -> 2, of which waited for: 3 -> 2; matrix products, arithmetic and copies ran while one was open for 0% -> 0% of each run, Pallas kernels for 0% -> 0%
where the time goes in v1:
time: 305 us
  waiting for transfers between devices  198 us (65%)
  blocking collectives  59.1 us (19%)
  starting transfers between devices  35.3 us (12%)
  Pallas kernels  7.66 us (3%)
    all_to_all x1, waiting for transfers between devices, shards(): raw = lax.all_to_all(snapshots.reshape(GROUPS, each, NFFT), 'freq', 0, 0)  192 us
    all_to_all x1, blocking collectives, shards(): mine = jnp.sum(lax.all_to_all(mine, 'freq', 0, 0), 0)  34.5 us
    all_to_all x1, starting transfers between devices, shards(): raw = lax.all_to_all(snapshots.reshape(GROUPS, each, NFFT), 'freq', 0, 0)  29.4 us
    all_to_all x1, blocking collectives, shards(): parts = lax.all_to_all(sums, 'space', 0, 0)  24.6 us
    pallas_call x1, Pallas kernels, gram_call(): pl.pallas_call(gram_kernel, out_shape=jax.ShapeDtypeStruct((GROUPS, FREQS...  6.37 us
  transfers between devices with their start and end apart: 2, of which 2 were waited for; matrix products, arithmetic and copies ran while one was open for 0% of the time, Pallas kernels for 0%

profile of v1, /device:TPU:1, one launch (start us, length us, event | category | flops | bytes accessed | tf_op | source)
XLA Modules:
  0.0 304.7 jit_solution(15391932954589661402)
XLA Ops:
  0.6 0.0 copy-start
  0.6 29.4 %all-to-all-start = ((bf16[32,128,256]{2,1,0:T(8,128)(2,1)}), bf16[32,128,256]{2,1,0:T(8,128)(2,1)S(1)}, u32[]{:S(2)}, u32[]{:S(2)}) async-start(bf16[32,128,256]{2,1,0:T(8,128)(2,1)} %bitcast.8), calls=%async_computation | async-start | bytes 4194304 | tf_op jit(solution)/shard_map/all_to_all | solution.py:194
  30.2 0.0 copy-done
  30.3 0.5 multiply_convert_fusion
  30.8 191.5 %all-to-all-done.raw_ref = bf16[32,128,256]{2,1,0:T(8,128)(2,1)S(1)} async-done(((bf16[32,128,256]{2,1,0:T(8,128)(2,1)}), bf16[32,128,256]{2,1,0:T(8,128)(2,1)S(1)}, u32[]{:S(2)}, u32[]{:S(2)}) %all-to-all-start) | async-done | bytes 2097184 | tf_op jit(solution)/shard_map/all_to_all | solution.py:194
  222.3 0.0 copy-start.1
  222.3 6.4 %gram.1 = bf16[32,128,128]{2,1,0:T(8,128)(2,1)S(1)} custom-call(f32[1]{0:T(128)} %bitcast.2.factor_ref, bf16[32,128,256]{2,1,0:T(8,128)(2,1)S(1)} %all-to-all-done.raw_ref, bf16[128,128]{1,0:T(8,128)(2,1)S(1)} %constant_dynamic-slice_fusion.tail_ref, bf16[256,256]{1,0:T(8,128)(2,1)S(1)} %pad_maximum_fusion.table_ref), custom_call_target="tpu_custom_call" | custom-call | tf_op jit(solution)/shard_map/gram/pallas_call | solution.py:87
  228.7 24.6 %all_to_all.20 = bf16[32,128,128]{2,1,0:T(8,128)(2,1)S(1)} all-to-all(bf16[32,128,128]{2,1,0:T(8,128)(2,1)S(1)} %gram.1), channel_id=1, replica_groups=mesh['space'=32,'freq'=32] {'space'}, dimensions={0} | all-to-all | bytes 2097152 | tf_op jit(solution)/shard_map/all_to_all | solution.py:199
  253.4 0.0 copy-done.1
  253.4 0.3 multiply_reduce_fusion
  253.6 34.5 %all_to_all.21 = f32[32,4,128]{2,1,0:T(4,128)S(1)} all-to-all(f32[32,4,128]{2,1,0:T(4,128)S(1)} %bitcast.9), channel_id=1, replica_groups=mesh['space'=32,'freq'=32] {'freq'}, dimensions={0} | all-to-all | bytes 131072 | tf_op jit(solution)/shard_map/all_to_all | solution.py:202
  288.2 0.6 broadcast_in_dim.2
  288.8 5.9 %all-to-all-start.3 = ((f32[32,4,128]{2,1,0:T(4,128)}), f32[32,4,128]{2,1,0:T(4,128)S(1)}, u32[]{:S(2)}, u32[]{:S(2)}) async-start(f32[32,4,128]{2,1,0:T(4,128)} %broadcast_in_dim.2), calls=%async_computation.3 | async-start | bytes 131072 | tf_op jit(solution)/shard_map/all_to_all | solution.py:203
  294.7 0.6 multiply_reduce_fusion.1
  296.0 6.0 %all-to-all-done.3.sums_ref = f32[32,4,128]{2,1,0:T(4,128)S(1)} async-done(((f32[32,4,128]{2,1,0:T(4,128)}), f32[32,4,128]{2,1,0:T(4,128)S(1)}, u32[]{:S(2)}, u32[]{:S(2)}) %all-to-all-start.3) | async-done | bytes 65568 | tf_op jit(solution)/shard_map/all_to_all | solution.py:203
  302.0 1.3 power.1
  303.3 0.1 reshape.41
  303.4 0.6 copy.12
  304.0 0.6 slice_reduce_fusion
  (5 shorter events, 0.2 us)
Async XLA Ops:
  0.6 29.6 %copy-start = (bf16[4096,128]{1,0:T(8,128)(2,1)S(1)}, bf16[4096,128]{1,0:T(8,128)(2,1)}, u32[]{:S(2)}) copy-start(bf16[4096,128]{1,0:T(8,128)(2,1)} %param.4) | copy-start | bytes 3145732
  0.6 221.7 %all-to-all-start = ((bf16[32,128,256]{2,1,0:T(8,128)(2,1)}), bf16[32,128,256]{2,1,0:T(8,128)(2,1)S(1)}, u32[]{:S(2)}, u32[]{:S(2)}) async-start(bf16[32,128,256]{2,1,0:T(8,128)(2,1)} %bitcast.8), calls=%async_computation | async-start | bytes 4194304 | tf_op jit(solution)/shard_map/all_to_all | solution.py:194
  222.3 31.0 %copy-start.1 = (f32[32]{0:T(128)S(1)}, f32[32]{0:T(128)}, u32[]{:S(2)}) copy-start(f32[32]{0:T(128)} %constant.53.clone) | copy-start | bytes 388
  288.8 13.2 %all-to-all-start.3 = ((f32[32,4,128]{2,1,0:T(4,128)}), f32[32,4,128]{2,1,0:T(4,128)S(1)}, u32[]{:S(2)}, u32[]{:S(2)}) async-start(f32[32,4,128]{2,1,0:T(4,128)} %broadcast_in_dim.2), calls=%async_computation.3 | async-start | bytes 131072 | tf_op jit(solution)/shard_map/all_to_all | solution.py:203

commit v2 on v1

--- a/solution.py
+++ b/solution.py
@@ -1,3 +1,4 @@
+import functools
 import math
 
 import jax
@@ -15,6 +16,7 @@
 FREQS = 128
 PITCH = 2 * FREQS + 8
 GROUPS = 32
+CHIPS = GROUPS // 2
 NT = (((1,), (1,)), ((), ()))
 
 
@@ -26,12 +28,10 @@
     table = jnp.concatenate(
         [window[None, :] * jnp.cos(phase), -window[None, :] * jnp.sin(phase)], 0
     )
-    return (table.astype(jnp.bfloat16), jnp.sum(window * window))
-
-
-def gram_kernel(factor_ref, raw_ref, tail_ref, table_ref, out_ref, coef_ref, sums_ref):
-    points = raw_ref.shape[1]
-
+    return table.astype(jnp.bfloat16)
+
+
+def gram_kernel(core_ref, raw_ref, tail_ref, table_ref, out_ref, coef_ref):
     def put(block, rows):
         coef = lax.dot_general(table_ref[...], rows, NT, preferred_element_type=jnp.float32)
         start = pl.multiple_of(block * PITCH, 8)
@@ -63,30 +63,26 @@
     def packed(f):
         return jnp.where(first, product(f, False), product(f + 1, True))
 
+    core = core_ref[0]
+
     def gram(step, carry):
         base = 8 * step
-        for core in range(2):
-            upper = packed(base + 2 * core)
-            lower = packed(base + 4 + 2 * core)
-            for chip in range(GROUPS // 2):
-                part = slice(4 * chip, 4 * chip + 4)
-                start = pl.multiple_of(base, 8)
-                sums_ref[2 * chip + core, pl.ds(start, 8), :] = jnp.concatenate(
-                    [upper[part], lower[part]], 0
-                )
+        upper = packed(base + 2 * core)
+        lower = packed(base + 4 + 2 * core)
+        start = pl.multiple_of(base, 8)
+        for chip in range(CHIPS):
+            part = slice(4 * chip, 4 * chip + 4)
+            out_ref[chip, pl.ds(start, 8), :] = jnp.concatenate([upper[part], lower[part]], 0)
         return carry
 
-    lax.fori_loop(0, FREQS // 8, gram, 0, unroll=2)
-    factor = factor_ref[0]
-    for index in range(GROUPS):
-        out_ref[index] = (sums_ref[index] * factor).astype(jnp.bfloat16)
-
-
-def gram_call(factor, raw, tail, table):
+    lax.fori_loop(0, FREQS // 8, gram, 0, unroll=4)
+
+
+def gram_call(core, raw, tail, table):
     points = raw.shape[1]
     return pl.pallas_call(
         gram_kernel,
-        out_shape=jax.ShapeDtypeStruct((GROUPS, FREQS, 2 * BLOCKS), jnp.bfloat16),
+        out_shape=jax.ShapeDtypeStruct((CHIPS, FREQS, 2 * BLOCKS), jnp.float32),
         in_specs=[
             pl.BlockSpec(memory_space=pltpu.SMEM),
             pl.BlockSpec(memory_space=pltpu.VMEM),
@@ -94,22 +90,18 @@
             pl.BlockSpec(memory_space=pltpu.VMEM),
         ],
         out_specs=pl.BlockSpec(memory_space=pltpu.VMEM),
-        scratch_shapes=[
-            pltpu.VMEM((BLOCKS * PITCH, points), jnp.float32),
-            pltpu.VMEM((GROUPS, FREQS, 2 * BLOCKS), jnp.float32),
-        ],
+        scratch_shapes=[pltpu.VMEM((BLOCKS * PITCH, points), jnp.float32)],
         compiler_params=pltpu.CompilerParams(vmem_limit_bytes=40 * 1024 * 1024),
         name="gram",
-    )(factor, raw, tail, table)
-
-
-def power_kernel(place_ref, scale_ref, sums_ref, rows_ref, spectrum_ref, matrix_ref):
-    scale = scale_ref[0]
+    )(core.reshape(1), raw, tail, table)
+
+
+def power_kernel(scale, place_ref, sums_ref, rows_ref, spectrum_ref, matrix_ref):
     row = lax.broadcasted_iota(jnp.int32, (BLOCKS, BLOCKS), 0)
     column = lax.broadcasted_iota(jnp.int32, (BLOCKS, BLOCKS), 1)
     matrices = []
     for core in range(2):
-        held = jnp.concatenate([sums_ref[2 * c + core] for c in range(GROUPS // 2)], 0) * scale
+        held = jnp.concatenate([sums_ref[2 * c + core] for c in range(CHIPS)], 0) * scale
         left, right = (held[:, :BLOCKS], held[:, BLOCKS:])
         left_t, right_t = (left.T, right.T)
         real_even = jnp.where(row <= column, left, left_t)
@@ -123,7 +115,9 @@
     matrix_ref[...] = matrix
     place = place_ref[0]
     for k in range(2):
-        rows_ref[:, k : k + 1, :] = matrix_ref[:, pl.ds(2 * place + k, 1), :]
+        line = matrix_ref[:, pl.ds(2 * place + k, 1), :]
+        rows_ref[:, 0, k : k + 1, :] = line[:, :, :BLOCKS]
+        rows_ref[:, 1, k : k + 1, :] = line[:, :, BLOCKS:]
 
     low = lax.broadcasted_iota(jnp.int32, (4, 1, 2 * BLOCKS), 2) < BLOCKS
     count = 2.0 * BLOCKS
@@ -159,29 +153,30 @@
     v_imag = jnp.sum(jnp.where(lane == line + BLOCKS, v, 0.0), axis=2, keepdims=True)
     top = jnp.sum(v_real * u_real + v_imag * u_imag, axis=1, keepdims=True) / count
     below = jnp.sum(v_real * v_real + v_imag * v_imag, axis=1, keepdims=True) / count
-    spectrum_ref[...] = jnp.broadcast_to(top / (below + 1e-06), spectrum_ref.shape)
+    ratio = top / (below + 1e-06)
+    for f in range(4):
+        spectrum_ref[f] = ratio[f, 0, 0]
 
 
 def power_call(place, scale, sums):
     return pl.pallas_call(
-        power_kernel,
+        functools.partial(power_kernel, scale),
         out_shape=(
-            jax.ShapeDtypeStruct((4, 2, 2 * BLOCKS), jnp.float32),
-            jax.ShapeDtypeStruct((4, 1, 2 * BLOCKS), jnp.float32),
+            jax.ShapeDtypeStruct((4, 2, 2, BLOCKS), jnp.float32),
+            jax.ShapeDtypeStruct((4,), jnp.float32),
         ),
         in_specs=[
             pl.BlockSpec(memory_space=pltpu.SMEM),
-            pl.BlockSpec(memory_space=pltpu.SMEM),
             pl.BlockSpec(memory_space=pltpu.VMEM),
         ],
         out_specs=(
             pl.BlockSpec(memory_space=pltpu.VMEM),
-            pl.BlockSpec(memory_space=pltpu.VMEM),
+            pl.BlockSpec(memory_space=pltpu.SMEM),
         ),
         scratch_shapes=[pltpu.VMEM((4, BLOCKS, 2 * BLOCKS), jnp.float32)],
         compiler_params=pltpu.CompilerParams(vmem_limit_bytes=16 * 1024 * 1024),
         name="power",
-    )(place, scale, sums)
+    )(place.reshape(1), sums)
 
 
 def shards(snapshots, tail):
@@ -189,20 +184,28 @@
     space = lax.axis_index("space")
     freq = lax.axis_index("freq")
     each = points // GROUPS
-    table, wsum = build_table()
-    scale = 1.0 / (points * GROUPS * wsum)
+    table = build_table()
+    scale = 1.0 / (points * GROUPS * (0.375 * NFFT))
     raw = lax.all_to_all(snapshots.reshape(GROUPS, each, NFFT), "freq", 0, 0)
     own_tail = lax.dynamic_slice_in_dim(tail, freq * each, each, 0)
-    factors = np.exp2(np.arange(GROUPS) / GROUPS).astype(np.float32)
-    factor = jnp.exp2(space.astype(jnp.float32) / GROUPS)
-    sums = gram_call(factor.reshape(1), raw, own_tail, table)
-    parts = lax.all_to_all(sums, "space", 0, 0)
-    undo = jnp.asarray(1.0 / factors, jnp.float32)[:, None, None]
+    core = space % 2
+    chip = space // 2
+    other = gram_call(1 - core, raw, own_tail, table)
+    other = lax.ppermute(other, "space", [(s, s ^ 1) for s in range(GROUPS)])
+    sums = gram_call(core, raw, own_tail, table) + other
+    factor = jnp.exp2(chip.astype(jnp.float32) / CHIPS)
+    undo = jnp.asarray(np.exp2(-np.arange(CHIPS) / CHIPS), jnp.float32)[:, None, None]
+    parts = lax.all_to_all(
+        (sums * factor).astype(jnp.bfloat16),
+        "space",
+        0,
+        0,
+        axis_index_groups=[[2 * i + c for i in range(CHIPS)] for c in range(2)],
+    )
     mine = jnp.sum(parts.astype(jnp.float32) * undo, 0).reshape(GROUPS, 4, 2 * BLOCKS)
     mine = jnp.sum(lax.all_to_all(mine, "freq", 0, 0), 0)
     whole = lax.all_to_all(jnp.broadcast_to(mine[None], (GROUPS,) + mine.shape), "space", 0, 0)
-    rows, spectrum = power_call(space.reshape(1), scale.reshape(1), whole)
-    return (rows.reshape(4, 2, 2, BLOCKS).transpose(0, 2, 1, 3), spectrum[:, 0, 0])
+    return power_call(space, scale, whole)
 
 
 def solution(mesh):

time: 305 us -> 303 us (level)
  waiting for transfers between devices: 198 us -> 192 us
  blocking collectives: 59.1 us -> 65.1 us
  Pallas kernels: 7.66 us -> 11.5 us
  starting transfers between devices: 35.3 us -> 31.9 us
    all_to_all x1 -> x2, blocking collectives: 24.6 us -> 31.6 us  [the longest x1 17.6 us: shards(): lax.all_to_all((sums * factor).astype(jnp.bfloat16), 'space', 0, 0, axis_...]
    all_to_all x1 -> x0, waiting for transfers between devices: 6.01 us -> none  [shards(): lax.all_to_all(jnp.broadcast_to(mine[None], (GROUPS,) + mine.shape), 'spa...]
    all_to_all x1 -> x0, starting transfers between devices: 5.89 us -> none  [shards(): lax.all_to_all(jnp.broadcast_to(mine[None], (GROUPS,) + mine.shape), 'spa...]
    pallas_call x2 -> x3, Pallas kernels: 7.66 us -> 11.5 us  [the longest x2 9.59 us: gram_call(): pl.pallas_call(gram_kernel, out_shape=jax.ShapeDtypeStruct((CHIPS, FREQS,...]
  transfers between devices with their start and end apart: 2 -> 2, of which waited for: 2 -> 1; matrix products, arithmetic and copies ran while one was open for 0% -> 0% of each run, Pallas kernels for 0% -> 1%
where the time goes in v2:
time: 303 us
  waiting for transfers between devices  192 us (63%)
  blocking collectives  65.1 us (21%)
  starting transfers between devices  31.9 us (11%)
  Pallas kernels  11.5 us (4%)
    all_to_all x1, waiting for transfers between devices, shards(): raw = lax.all_to_all(snapshots.reshape(GROUPS, each, NFFT), 'freq', 0, 0)  192 us
    all_to_all x1, blocking collectives, shards(): mine = jnp.sum(lax.all_to_all(mine, 'freq', 0, 0), 0)  33.4 us
    all_to_all x1, starting transfers between devices, shards(): raw = lax.all_to_all(snapshots.reshape(GROUPS, each, NFFT), 'freq', 0, 0)  29.4 us
    all_to_all x1, blocking collectives, shards(): lax.all_to_all((sums * factor).astype(jnp.bfloat16), 'space', 0, 0, axis_...  17.6 us
    all_to_all x1, blocking collectives, shards(): lax.all_to_all(jnp.broadcast_to(mine[None], (GROUPS,) + mine.shape), 'spa...  14 us
    pallas_call x2, Pallas kernels, gram_call(): pl.pallas_call(gram_kernel, out_shape=jax.ShapeDtypeStruct((CHIPS, FREQS,...  9.59 us
  transfers between devices with their start and end apart: 2, of which 1 were waited for; matrix products, arithmetic and copies ran while one was open for 0% of the time, Pallas kernels for 1%

profile of v2, /device:TPU:1, one launch (start us, length us, event | category | flops | bytes accessed | tf_op | source)
XLA Modules:
  0.0 303.0 jit_solution(13677593196136612879)
XLA Ops:
  0.6 0.0 copy-start
  0.6 29.4 %all-to-all-start = ((bf16[32,128,256]{2,1,0:T(8,128)(2,1)}), bf16[32,128,256]{2,1,0:T(8,128)(2,1)S(1)}, u32[]{:S(2)}, u32[]{:S(2)}) async-start(bf16[32,128,256]{2,1,0:T(8,128)(2,1)} %bitcast.5), calls=%async_computation | async-start | bytes 4194304 | tf_op jit(solution)/shard_map/all_to_all | solution.py:189
  30.2 0.0 copy-done
  30.2 0.5 multiply_convert_fusion.1
  30.8 191.6 %all-to-all-done.raw_ref = bf16[32,128,256]{2,1,0:T(8,128)(2,1)S(1)} async-done(((bf16[32,128,256]{2,1,0:T(8,128)(2,1)}), bf16[32,128,256]{2,1,0:T(8,128)(2,1)S(1)}, u32[]{:S(2)}, u32[]{:S(2)}) %all-to-all-start) | async-done | bytes 2097184 | tf_op jit(solution)/shard_map/all_to_all | solution.py:189
  222.3 5.3 %gram.3 = f32[16,128,128]{2,1,0:T(8,128)} custom-call(s32[1]{0:T(128)} %bitcast.3.core_ref, bf16[32,128,256]{2,1,0:T(8,128)(2,1)S(1)} %all-to-all-done.raw_ref, bf16[128,128]{1,0:T(8,128)(2,1)S(1)} %constant_dynamic-slice_fusion.tail_ref, bf16[256,256]{1,0:T(8,128)(2,1)S(1)} %pad_maximum_fusion.table_ref), custom_call_target="tpu_custom_call" | custom-call | tf_op jit(solution)/shard_map/gram/pallas_call | solution.py:83
  227.6 2.5 collective-permute-start
  230.2 4.3 %gram.2 = f32[16,128,128]{2,1,0:T(8,128)S(1)} custom-call(s32[1]{0:T(128)} %bitcast.1.core_ref, bf16[32,128,256]{2,1,0:T(8,128)(2,1)S(1)} %all-to-all-done.raw_ref, bf16[128,128]{1,0:T(8,128)(2,1)S(1)} %constant_dynamic-slice_fusion.tail_ref, bf16[256,256]{1,0:T(8,128)(2,1)S(1)} %pad_maximum_fusion.table_ref), custom_call_target="tpu_custom_call" | custom-call | tf_op jit(solution)/shard_map/gram/pallas_call | solution.py:83
  234.5 0.0 copy-start.1
  234.5 0.0 collective-permute-done
  234.5 1.4 multiply_convert_fusion
  235.9 17.6 %all_to_all.20 = bf16[16,128,128]{2,1,0:T(8,128)(2,1)S(1)} all-to-all(bf16[16,128,128]{2,1,0:T(8,128)(2,1)S(1)} %multiply_convert_fusion), channel_id=1, replica_groups={{0,64,128,192,256,320,384,448,512,576,640,704,768,832,896,960},{32,96,1..., dimensions={0} | all-to-all | bytes 1048576 | tf_op jit(solution)/shard_map/all_to_all | solution.py:198
  253.5 0.0 copy-done.1
  253.5 0.2 multiply_reduce_fusion
  253.7 33.4 %all_to_all.21 = f32[32,4,128]{2,1,0:T(4,128)S(1)} all-to-all(f32[32,4,128]{2,1,0:T(4,128)S(1)} %bitcast.6), channel_id=1, replica_groups=mesh['space'=32,'freq'=32] {'freq'}, dimensions={0} | all-to-all | bytes 131072 | tf_op jit(solution)/shard_map/all_to_all | solution.py:206
  287.1 14.0 %all_to_all.22.sums_ref = f32[32,4,128]{2,1,0:T(4,128)S(1)} all-to-all(f32[32,4,128]{2,1,0:T(4,128)S(1)} %broadcast_in_dim.2), channel_id=1, replica_groups=mesh['space'=32,'freq'=32] {'space'}, dimensions={0} | all-to-all | bytes 131072 | tf_op jit(solution)/shard_map/all_to_all | solution.py:207
  301.2 1.9 power.1
  (6 shorter events, 0.2 us)
Async XLA Ops:
  0.6 29.6 %copy-start = (bf16[4096,128]{1,0:T(8,128)(2,1)S(1)}, bf16[4096,128]{1,0:T(8,128)(2,1)}, u32[]{:S(2)}) copy-start(bf16[4096,128]{1,0:T(8,128)(2,1)} %param.4) | copy-start | bytes 3145732
  0.6 221.7 %all-to-all-start = ((bf16[32,128,256]{2,1,0:T(8,128)(2,1)}), bf16[32,128,256]{2,1,0:T(8,128)(2,1)S(1)}, u32[]{:S(2)}, u32[]{:S(2)}) async-start(bf16[32,128,256]{2,1,0:T(8,128)(2,1)} %bitcast.5), calls=%async_computation | async-start | bytes 4194304 | tf_op jit(solution)/shard_map/all_to_all | solution.py:189
  227.6 6.9 %collective-permute-start = (f32[16,128,128]{2,1,0:T(8,128)}, f32[16,128,128]{2,1,0:T(8,128)}, u32[]{:S(2)}, u32[]{:S(2)}) collective-permute-start(f32[16,128,128]{2,1,0:T(8,128)} %gram.3), channel_id=1, source_target_pairs={{0,32},{32,0},{64,96},{96,64},{128,160},{160,128},{192,224},{224,1... | collective-permute-start | bytes 3145736 | tf_op jit(solution)/shard_map/ppermute | solution.py:194
  234.5 19.0 %copy-start.1 = (f32[16]{0:T(128)S(1)}, f32[16]{0:T(128)}, u32[]{:S(2)}) copy-start(f32[16]{0:T(128)} %constant.72.clone) | copy-start | bytes 196

commit v3 on v2

--- a/solution.py
+++ b/solution.py
@@ -17,6 +17,8 @@
 PITCH = 2 * FREQS + 8
 GROUPS = 32
 CHIPS = GROUPS // 2
+ORDER = [int(format(r, "05b")[::-1], 2) for r in range(GROUPS)]
+RANK = [ORDER.index(z) for z in range(GROUPS)]
 NT = (((1,), (1,)), ((), ()))
 
 
@@ -34,19 +36,13 @@
 def gram_kernel(core_ref, raw_ref, tail_ref, table_ref, out_ref, coef_ref):
     def put(block, rows):
         coef = lax.dot_general(table_ref[...], rows, NT, preferred_element_type=jnp.float32)
-        start = pl.multiple_of(block * PITCH, 8)
-        coef_ref[pl.ds(start, 2 * FREQS), :] = coef
-
-    def transform(z, carry):
-        rows = raw_ref[z]
+        coef_ref[pl.ds(block * PITCH, 2 * FREQS), :] = coef
+
+    for z in range(GROUPS):
+        rows = raw_ref[RANK[z]]
+        after = tail_ref[...] if z == GROUPS - 1 else raw_ref[RANK[z + 1]][:, :HALF]
         put(2 * z, rows)
-        put(2 * z + 1, jnp.concatenate([rows[:, HALF:], raw_ref[z + 1][:, :HALF]], 1))
-        return carry
-
-    lax.fori_loop(0, GROUPS - 1, transform, 0, unroll=True)
-    rows = raw_ref[GROUPS - 1]
-    put(2 * GROUPS - 2, rows)
-    put(2 * GROUPS - 1, jnp.concatenate([rows[:, HALF:], tail_ref[...]], 1))
+        put(2 * z + 1, jnp.concatenate([rows[:, HALF:], after], 1))
 
     row = lax.broadcasted_iota(jnp.int32, (BLOCKS, 2 * BLOCKS), 0)
     lane = lax.broadcasted_iota(jnp.int32, (BLOCKS, 2 * BLOCKS), 1)
@@ -91,7 +87,7 @@
         ],
         out_specs=pl.BlockSpec(memory_space=pltpu.VMEM),
         scratch_shapes=[pltpu.VMEM((BLOCKS * PITCH, points), jnp.float32)],
-        compiler_params=pltpu.CompilerParams(vmem_limit_bytes=40 * 1024 * 1024),
+        compiler_params=pltpu.CompilerParams(vmem_limit_bytes=16 * 1024 * 1024),
         name="gram",
     )(core.reshape(1), raw, tail, table)
 
@@ -186,8 +182,11 @@
     each = points // GROUPS
     table = build_table()
     scale = 1.0 / (points * GROUPS * (0.375 * NFFT))
-    raw = lax.all_to_all(snapshots.reshape(GROUPS, each, NFFT), "freq", 0, 0)
-    own_tail = lax.dynamic_slice_in_dim(tail, freq * each, each, 0)
+    raw = lax.all_to_all(
+        snapshots.reshape(GROUPS, each, NFFT), "freq", 0, 0, axis_index_groups=[ORDER]
+    )
+    rank = sum(((freq >> bit) & 1) << (4 - bit) for bit in range(5))
+    own_tail = lax.dynamic_slice_in_dim(tail, rank * each, each, 0)
     core = space % 2
     chip = space // 2
     other = gram_call(1 - core, raw, own_tail, table)

time: 303 us -> 304 us (level)
  waiting for transfers between devices: 192 us -> 187 us
  starting transfers between devices: 31.9 us -> 35.9 us
    all_to_all x1, waiting for transfers between devices: 192 us -> 187 us  [shards(): lax.all_to_all(snapshots.reshape(GROUPS, each, NFFT), 'freq', 0, 0, axis_...]
    ppermute x1, starting transfers between devices: 2.48 us -> 6.43 us  [shards(): other = lax.ppermute(other, 'space', [(s, s ^ 1) for s in range(GROUPS)])]
where the time goes in v3:
time: 304 us
  waiting for transfers between devices  187 us (62%)
  blocking collectives  66.5 us (22%)
  starting transfers between devices  35.9 us (12%)
  Pallas kernels  11.5 us (4%)
    all_to_all x1, waiting for transfers between devices, shards(): lax.all_to_all(snapshots.reshape(GROUPS, each, NFFT), 'freq', 0, 0, axis_...  187 us
    all_to_all x1, blocking collectives, shards(): mine = jnp.sum(lax.all_to_all(mine, 'freq', 0, 0), 0)  34.9 us
    all_to_all x1, starting transfers between devices, shards(): lax.all_to_all(snapshots.reshape(GROUPS, each, NFFT), 'freq', 0, 0, axis_...  29.4 us
    all_to_all x1, blocking collectives, shards(): lax.all_to_all((sums * factor).astype(jnp.bfloat16), 'space', 0, 0, axis_...  17.6 us
    all_to_all x1, blocking collectives, shards(): lax.all_to_all(jnp.broadcast_to(mine[None], (GROUPS,) + mine.shape), 'spa...  14 us
    pallas_call x2, Pallas kernels, gram_call(): pl.pallas_call(gram_kernel, out_shape=jax.ShapeDtypeStruct((CHIPS, FREQS,...  9.59 us
    ppermute x1, starting transfers between devices, shards(): other = lax.ppermute(other, 'space', [(s, s ^ 1) for s in range(GROUPS)])  6.43 us
  transfers between devices with their start and end apart: 2, of which 1 were waited for; matrix products, arithmetic and copies ran while one was open for 0% of the time, Pallas kernels for 1%

profile of v3, /device:TPU:1, one launch (start us, length us, event | category | flops | bytes accessed | tf_op | source)
XLA Modules:
  0.0 304.0 jit_solution(17219188454996548935)
XLA Ops:
  0.6 0.0 copy-start
  0.6 29.4 %all-to-all-start = ((bf16[32,128,256]{2,1,0:T(8,128)(2,1)}), bf16[32,128,256]{2,1,0:T(8,128)(2,1)S(1)}, u32[]{:S(2)}, u32[]{:S(2)}) async-start(bf16[32,128,256]{2,1,0:T(8,128)(2,1)} %bitcast.5), calls=%async_computation | async-start | bytes 4194304 | tf_op jit(solution)/shard_map/all_to_all | solution.py:185
  30.2 0.0 copy-done
  30.2 0.5 multiply_convert_fusion.1
  30.8 187.1 %all-to-all-done.raw_ref = bf16[32,128,256]{2,1,0:T(8,128)(2,1)S(1)} async-done(((bf16[32,128,256]{2,1,0:T(8,128)(2,1)}), bf16[32,128,256]{2,1,0:T(8,128)(2,1)S(1)}, u32[]{:S(2)}, u32[]{:S(2)}) %all-to-all-start) | async-done | bytes 2097184 | tf_op jit(solution)/shard_map/all_to_all | solution.py:185
  217.9 5.3 %gram.3 = f32[16,128,128]{2,1,0:T(8,128)} custom-call(s32[1]{0:T(128)} %bitcast.3.core_ref, bf16[32,128,256]{2,1,0:T(8,128)(2,1)S(1)} %all-to-all-done.raw_ref, bf16[128,128]{1,0:T(8,128)(2,1)S(1)} %constant_dynamic-slice_fusion.tail_ref, bf16[256,256]{1,0:T(8,128)(2,1)S(1)} %pad_maximum_fusion.table_ref), custom_call_target="tpu_custom_call" | custom-call | tf_op jit(solution)/shard_map/gram/pallas_call | solution.py:79
  223.2 6.4 %collective-permute-start = (f32[16,128,128]{2,1,0:T(8,128)}, f32[16,128,128]{2,1,0:T(8,128)}, u32[]{:S(2)}, u32[]{:S(2)}) collective-permute-start(f32[16,128,128]{2,1,0:T(8,128)} %gram.3), channel_id=1, source_target_pairs={{0,32},{32,0},{64,96},{96,64},{128,160},{160,128},{192,224},{224,1... | collective-permute-start | bytes 3145736 | tf_op jit(solution)/shard_map/ppermute | solution.py:193
  229.7 4.3 %gram.2 = f32[16,128,128]{2,1,0:T(8,128)S(1)} custom-call(s32[1]{0:T(128)} %bitcast.1.core_ref, bf16[32,128,256]{2,1,0:T(8,128)(2,1)S(1)} %all-to-all-done.raw_ref, bf16[128,128]{1,0:T(8,128)(2,1)S(1)} %constant_dynamic-slice_fusion.tail_ref, bf16[256,256]{1,0:T(8,128)(2,1)S(1)} %pad_maximum_fusion.table_ref), custom_call_target="tpu_custom_call" | custom-call | tf_op jit(solution)/shard_map/gram/pallas_call | solution.py:79
  234.0 0.0 copy-start.1
  234.0 0.0 collective-permute-done
  234.1 1.4 multiply_convert_fusion
  235.4 17.6 %all_to_all.20 = bf16[16,128,128]{2,1,0:T(8,128)(2,1)S(1)} all-to-all(bf16[16,128,128]{2,1,0:T(8,128)(2,1)S(1)} %multiply_convert_fusion), channel_id=1, replica_groups={{0,64,128,192,256,320,384,448,512,576,640,704,768,832,896,960},{32,96,1..., dimensions={0} | all-to-all | bytes 1048576 | tf_op jit(solution)/shard_map/all_to_all | solution.py:197
  253.1 0.0 copy-done.1
  253.1 0.2 multiply_reduce_fusion
  253.2 34.9 %all_to_all.21 = f32[32,4,128]{2,1,0:T(4,128)S(1)} all-to-all(f32[32,4,128]{2,1,0:T(4,128)S(1)} %bitcast.6), channel_id=1, replica_groups=mesh['space'=32,'freq'=32] {'freq'}, dimensions={0} | all-to-all | bytes 131072 | tf_op jit(solution)/shard_map/all_to_all | solution.py:205
  288.2 14.0 %all_to_all.22.sums_ref = f32[32,4,128]{2,1,0:T(4,128)S(1)} all-to-all(f32[32,4,128]{2,1,0:T(4,128)S(1)} %broadcast_in_dim.2), channel_id=1, replica_groups=mesh['space'=32,'freq'=32] {'space'}, dimensions={0} | all-to-all | bytes 131072 | tf_op jit(solution)/shard_map/all_to_all | solution.py:206
  302.2 1.9 power.1
  (6 shorter events, 0.2 us)
Async XLA Ops:
  0.6 29.6 %copy-start = (bf16[4096,128]{1,0:T(8,128)(2,1)S(1)}, bf16[4096,128]{1,0:T(8,128)(2,1)}, u32[]{:S(2)}) copy-start(bf16[4096,128]{1,0:T(8,128)(2,1)} %param.4) | copy-start | bytes 3145732
  0.6 217.3 %all-to-all-start = ((bf16[32,128,256]{2,1,0:T(8,128)(2,1)}), bf16[32,128,256]{2,1,0:T(8,128)(2,1)S(1)}, u32[]{:S(2)}, u32[]{:S(2)}) async-start(bf16[32,128,256]{2,1,0:T(8,128)(2,1)} %bitcast.5), calls=%async_computation | async-start | bytes 4194304 | tf_op jit(solution)/shard_map/all_to_all | solution.py:185
  223.2 10.8 %collective-permute-start = (f32[16,128,128]{2,1,0:T(8,128)}, f32[16,128,128]{2,1,0:T(8,128)}, u32[]{:S(2)}, u32[]{:S(2)}) collective-permute-start(f32[16,128,128]{2,1,0:T(8,128)} %gram.3), channel_id=1, source_target_pairs={{0,32},{32,0},{64,96},{96,64},{128,160},{160,128},{192,224},{224,1... | collective-permute-start | bytes 3145736 | tf_op jit(solution)/shard_map/ppermute | solution.py:193
  234.0 19.0 %copy-start.1 = (f32[16]{0:T(128)S(1)}, f32[16]{0:T(128)}, u32[]{:S(2)}) copy-start(f32[16]{0:T(128)} %constant.76.clone) | copy-start | bytes 196

commit v4 on v3

--- a/solution.py
+++ b/solution.py
@@ -17,8 +17,6 @@
 PITCH = 2 * FREQS + 8
 GROUPS = 32
 CHIPS = GROUPS // 2
-ORDER = [int(format(r, "05b")[::-1], 2) for r in range(GROUPS)]
-RANK = [ORDER.index(z) for z in range(GROUPS)]
 NT = (((1,), (1,)), ((), ()))
 
 
@@ -33,14 +31,14 @@
     return table.astype(jnp.bfloat16)
 
 
-def gram_kernel(core_ref, raw_ref, tail_ref, table_ref, out_ref, coef_ref):
+def gram_kernel(unroll, core_ref, factor_ref, raw_ref, tail_ref, table_ref, own_ref, other_ref, coef_ref, held_ref):
     def put(block, rows):
         coef = lax.dot_general(table_ref[...], rows, NT, preferred_element_type=jnp.float32)
         coef_ref[pl.ds(block * PITCH, 2 * FREQS), :] = coef
 
     for z in range(GROUPS):
-        rows = raw_ref[RANK[z]]
-        after = tail_ref[...] if z == GROUPS - 1 else raw_ref[RANK[z + 1]][:, :HALF]
+        rows = raw_ref[z]
+        after = tail_ref[...] if z == GROUPS - 1 else raw_ref[z + 1][:, :HALF]
         put(2 * z, rows)
         put(2 * z + 1, jnp.concatenate([rows[:, HALF:], after], 1))
 
@@ -61,35 +59,53 @@
 
     core = core_ref[0]
 
-    def gram(step, carry):
-        base = 8 * step
-        upper = packed(base + 2 * core)
-        lower = packed(base + 4 + 2 * core)
-        start = pl.multiple_of(base, 8)
-        for chip in range(CHIPS):
-            part = slice(4 * chip, 4 * chip + 4)
-            out_ref[chip, pl.ds(start, 8), :] = jnp.concatenate([upper[part], lower[part]], 0)
-        return carry
-
-    lax.fori_loop(0, FREQS // 8, gram, 0, unroll=4)
-
-
-def gram_call(core, raw, tail, table):
+    def half(target_ref, core):
+        def gram(step, carry):
+            base = 8 * step
+            upper = packed(base + 2 * core)
+            lower = packed(base + 4 + 2 * core)
+            start = pl.multiple_of(base, 8)
+            for chip in range(CHIPS):
+                part = slice(4 * chip, 4 * chip + 4)
+                target_ref[chip, pl.ds(start, 8), :] = jnp.concatenate(
+                    [upper[part], lower[part]], 0
+                )
+            return carry
+
+        lax.fori_loop(0, FREQS // 8, gram, 0, unroll=unroll)
+
+    half(held_ref, 1 - core)
+    other_ref[...] = (held_ref[...] * factor_ref[0]).astype(jnp.bfloat16)
+    half(own_ref, core)
+
+
+def gram_call(core, factor, raw, tail, table, unroll=16):
     points = raw.shape[1]
+    shape = (CHIPS, FREQS, 2 * BLOCKS)
     return pl.pallas_call(
-        gram_kernel,
-        out_shape=jax.ShapeDtypeStruct((CHIPS, FREQS, 2 * BLOCKS), jnp.float32),
+        functools.partial(gram_kernel, unroll),
+        out_shape=(
+            jax.ShapeDtypeStruct(shape, jnp.float32),
+            jax.ShapeDtypeStruct(shape, jnp.bfloat16),
+        ),
         in_specs=[
             pl.BlockSpec(memory_space=pltpu.SMEM),
+            pl.BlockSpec(memory_space=pltpu.SMEM),
             pl.BlockSpec(memory_space=pltpu.VMEM),
             pl.BlockSpec(memory_space=pltpu.VMEM),
             pl.BlockSpec(memory_space=pltpu.VMEM),
         ],
-        out_specs=pl.BlockSpec(memory_space=pltpu.VMEM),
-        scratch_shapes=[pltpu.VMEM((BLOCKS * PITCH, points), jnp.float32)],
-        compiler_params=pltpu.CompilerParams(vmem_limit_bytes=16 * 1024 * 1024),
+        out_specs=(
+            pl.BlockSpec(memory_space=pltpu.VMEM),
+            pl.BlockSpec(memory_space=pltpu.VMEM),
+        ),
+        scratch_shapes=[
+            pltpu.VMEM((BLOCKS * PITCH, points), jnp.float32),
+            pltpu.VMEM(shape, jnp.float32),
+        ],
+        compiler_params=pltpu.CompilerParams(vmem_limit_bytes=20 * 1024 * 1024),
         name="gram",
-    )(core.reshape(1), raw, tail, table)
+    )(core.reshape(1), factor.reshape(1), raw, tail, table)
 
 
 def power_kernel(scale, place_ref, sums_ref, rows_ref, spectrum_ref, matrix_ref):
@@ -182,20 +198,17 @@
     each = points // GROUPS
     table = build_table()
     scale = 1.0 / (points * GROUPS * (0.375 * NFFT))
-    raw = lax.all_to_all(
-        snapshots.reshape(GROUPS, each, NFFT), "freq", 0, 0, axis_index_groups=[ORDER]
-    )
-    rank = sum(((freq >> bit) & 1) << (4 - bit) for bit in range(5))
-    own_tail = lax.dynamic_slice_in_dim(tail, rank * each, each, 0)
+    raw = lax.all_to_all(snapshots.reshape(GROUPS, each, NFFT), "freq", 0, 0)
+    own_tail = lax.dynamic_slice_in_dim(tail, freq * each, each, 0)
     core = space % 2
     chip = space // 2
-    other = gram_call(1 - core, raw, own_tail, table)
+    factor = jnp.exp2(chip.astype(jnp.float32) / CHIPS)
+    own, other = gram_call(core, factor, raw, own_tail, table)
     other = lax.ppermute(other, "space", [(s, s ^ 1) for s in range(GROUPS)])
-    sums = gram_call(core, raw, own_tail, table) + other
-    factor = jnp.exp2(chip.astype(jnp.float32) / CHIPS)
+    sums = own * factor + other.astype(jnp.float32)
     undo = jnp.asarray(np.exp2(-np.arange(CHIPS) / CHIPS), jnp.float32)[:, None, None]
     parts = lax.all_to_all(
-        (sums * factor).astype(jnp.bfloat16),
+        sums.astype(jnp.bfloat16),
         "space",
         0,
         0,

time: 304 us -> 299 us (0.984)
  waiting for transfers between devices: 187 us -> 193 us
  Pallas kernels: 11.5 us -> 7.24 us
  starting transfers between devices: 35.9 us -> 31.9 us
    all_to_all x1, waiting for transfers between devices: 187 us -> 192 us  [shards(): raw = lax.all_to_all(snapshots.reshape(GROUPS, each, NFFT), 'freq', 0, 0)]
    pallas_call x2 -> x1, Pallas kernels: 9.59 us -> 5.38 us  [gram_call(): pl.pallas_call(functools.partial(gram_kernel, unroll), out_shape=(jax.Sha...]
    ppermute x1, starting transfers between devices: 6.43 us -> 2.49 us  [shards(): other = lax.ppermute(other, 'space', [(s, s ^ 1) for s in range(GROUPS)])]
  transfers between devices with their start and end apart: 2 -> 2, of which waited for: 1 -> 2; matrix products, arithmetic and copies ran while one was open for 0% -> 0% of each run, Pallas kernels for 1% -> 0%
where the time goes in v4:
time: 299 us
  waiting for transfers between devices  193 us (65%)
  blocking collectives  64.9 us (22%)
  starting transfers between devices  31.9 us (11%)
  Pallas kernels  7.24 us (2%)
    all_to_all x1, waiting for transfers between devices, shards(): raw = lax.all_to_all(snapshots.reshape(GROUPS, each, NFFT), 'freq', 0, 0)  192 us
    all_to_all x1, blocking collectives, shards(): mine = jnp.sum(lax.all_to_all(mine, 'freq', 0, 0), 0)  33.5 us
    all_to_all x1, starting transfers between devices, shards(): raw = lax.all_to_all(snapshots.reshape(GROUPS, each, NFFT), 'freq', 0, 0)  29.4 us
    all_to_all x1, blocking collectives, shards(): lax.all_to_all(sums.astype(jnp.bfloat16), 'space', 0, 0, axis_index_group...  17.3 us
    all_to_all x1, blocking collectives, shards(): lax.all_to_all(jnp.broadcast_to(mine[None], (GROUPS,) + mine.shape), 'spa...  14.2 us
  transfers between devices with their start and end apart: 2, of which 2 were waited for; matrix products, arithmetic and copies ran while one was open for 0% of the time, Pallas kernels for 0%

profile of v4, /device:TPU:1, one launch (start us, length us, event | category | flops | bytes accessed | tf_op | source)
XLA Modules:
  0.0 298.9 jit_solution(17010807870175755889)
XLA Ops:
  0.6 0.0 copy-start
  0.6 29.4 %all-to-all-start = ((bf16[32,128,256]{2,1,0:T(8,128)(2,1)}), bf16[32,128,256]{2,1,0:T(8,128)(2,1)S(1)}, u32[]{:S(2)}, u32[]{:S(2)}) async-start(bf16[32,128,256]{2,1,0:T(8,128)(2,1)} %bitcast.5), calls=%async_computation | async-start | bytes 4194304 | tf_op jit(solution)/shard_map/all_to_all | solution.py:201
  30.2 0.0 copy-done
  30.3 0.5 multiply_convert_fusion
  30.8 191.5 %all-to-all-done.raw_ref = bf16[32,128,256]{2,1,0:T(8,128)(2,1)S(1)} async-done(((bf16[32,128,256]{2,1,0:T(8,128)(2,1)}), bf16[32,128,256]{2,1,0:T(8,128)(2,1)S(1)}, u32[]{:S(2)}, u32[]{:S(2)}) %all-to-all-start) | async-done | bytes 2097184 | tf_op jit(solution)/shard_map/all_to_all | solution.py:201
  222.3 5.4 %gram.1 = (f32[16,128,128]{2,1,0:T(8,128)S(1)}, bf16[16,128,128]{2,1,0:T(8,128)(2,1)S(1)}) custom-call(s32[1]{0:T(128)} %bitcast.1.core_ref, f32[1]{0:T(128)} %bitcast.2.factor_ref, bf16[32,128,256]{2,1,0:T(8,128)(2,1)S(1)} %all-to-all-done.raw_ref, bf16[128,128]{1,0:T(8,128)(2,1)S(1)} %constant_dynamic-slice_fusion.tail_ref, ...), custom_call_target="tpu_custom_call" | custom-call | tf_op jit(solution)/shard_map/gram/pallas_call | solution.py:85
  227.7 0.0 copy-start.1
  227.7 2.5 collective-permute-start
  230.2 1.5 collective-permute-done
  231.8 0.1 add_convert_fusion
  231.9 17.3 %all_to_all.20 = bf16[16,128,128]{2,1,0:T(8,128)(2,1)S(1)} all-to-all(bf16[16,128,128]{2,1,0:T(8,128)(2,1)S(1)} %add_convert_fusion), channel_id=1, replica_groups={{0,64,128,192,256,320,384,448,512,576,640,704,768,832,896,960},{32,96,1..., dimensions={0} | all-to-all | bytes 1048576 | tf_op jit(solution)/shard_map/all_to_all | solution.py:210
  249.2 0.0 copy-done.1
  249.2 0.2 multiply_reduce_fusion
  249.3 33.5 %all_to_all.21 = f32[32,4,128]{2,1,0:T(4,128)S(1)} all-to-all(f32[32,4,128]{2,1,0:T(4,128)S(1)} %bitcast.6), channel_id=1, replica_groups=mesh['space'=32,'freq'=32] {'freq'}, dimensions={0} | all-to-all | bytes 131072 | tf_op jit(solution)/shard_map/all_to_all | solution.py:218
  282.9 14.2 %all_to_all.22.sums_ref = f32[32,4,128]{2,1,0:T(4,128)S(1)} all-to-all(f32[32,4,128]{2,1,0:T(4,128)S(1)} %broadcast_in_dim.2), channel_id=1, replica_groups=mesh['space'=32,'freq'=32] {'space'}, dimensions={0} | all-to-all | bytes 131072 | tf_op jit(solution)/shard_map/all_to_all | solution.py:219
  297.1 1.9 power.1
  (6 shorter events, 0.2 us)
Async XLA Ops:
  0.6 29.6 %copy-start = (bf16[4096,128]{1,0:T(8,128)(2,1)S(1)}, bf16[4096,128]{1,0:T(8,128)(2,1)}, u32[]{:S(2)}) copy-start(bf16[4096,128]{1,0:T(8,128)(2,1)} %param.4) | copy-start | bytes 3145732
  0.6 221.7 %all-to-all-start = ((bf16[32,128,256]{2,1,0:T(8,128)(2,1)}), bf16[32,128,256]{2,1,0:T(8,128)(2,1)S(1)}, u32[]{:S(2)}, u32[]{:S(2)}) async-start(bf16[32,128,256]{2,1,0:T(8,128)(2,1)} %bitcast.5), calls=%async_computation | async-start | bytes 4194304 | tf_op jit(solution)/shard_map/all_to_all | solution.py:201
  227.7 21.4 %copy-start.1 = (f32[16]{0:T(128)S(1)}, f32[16]{0:T(128)}, u32[]{:S(2)}) copy-start(f32[16]{0:T(128)} %constant.71.clone) | copy-start | bytes 196
  227.7 4.0 %collective-permute-start = (bf16[16,128,128]{2,1,0:T(8,128)(2,1)S(1)}, bf16[16,128,128]{2,1,0:T(8,128)(2,1)S(1)}, u32[]{:S(2)}, u32[]{:S(2)}) collective-permute-start(bf16[16,128,128]{2,1,0:T(8,128)(2,1)S(1)} %get-tuple-element.5), channel_id=1, source_target_pairs={{0,32},{32,0},{64,96},{96,64},{128,160},{160,128},{192,224},{224,1... | collective-permute-start | bytes 1572872 | tf_op jit(solution)/shard_map/ppermute | solution.py:207

commit v5 on v4

--- a/solution.py
+++ b/solution.py
@@ -17,6 +17,8 @@
 PITCH = 2 * FREQS + 8
 GROUPS = 32
 CHIPS = GROUPS // 2
+ORDER = [(r % 4) * 8 + r // 4 for r in range(GROUPS)]
+RANK = [ORDER.index(z) for z in range(GROUPS)]
 NT = (((1,), (1,)), ((), ()))
 
 
@@ -37,8 +39,8 @@
         coef_ref[pl.ds(block * PITCH, 2 * FREQS), :] = coef
 
     for z in range(GROUPS):
-        rows = raw_ref[z]
-        after = tail_ref[...] if z == GROUPS - 1 else raw_ref[z + 1][:, :HALF]
+        rows = raw_ref[RANK[z]]
+        after = tail_ref[...] if z == GROUPS - 1 else raw_ref[RANK[z + 1]][:, :HALF]
         put(2 * z, rows)
         put(2 * z + 1, jnp.concatenate([rows[:, HALF:], after], 1))
 
@@ -198,8 +200,11 @@
     each = points // GROUPS
     table = build_table()
     scale = 1.0 / (points * GROUPS * (0.375 * NFFT))
-    raw = lax.all_to_all(snapshots.reshape(GROUPS, each, NFFT), "freq", 0, 0)
-    own_tail = lax.dynamic_slice_in_dim(tail, freq * each, each, 0)
+    raw = lax.all_to_all(
+        snapshots.reshape(GROUPS, each, NFFT), "freq", 0, 0, axis_index_groups=[ORDER]
+    )
+    rank = (freq % 8) * 4 + freq // 8
+    own_tail = lax.dynamic_slice_in_dim(tail, rank * each, each, 0)
     core = space % 2
     chip = space // 2
     factor = jnp.exp2(chip.astype(jnp.float32) / CHIPS)

time: 299 us -> 299 us (level)
  waiting for transfers between devices: 193 us -> 177 us
  blocking collectives: 64.9 us -> 76.4 us
  starting transfers between devices: 31.9 us -> 36.4 us
    all_to_all x1, waiting for transfers between devices: 192 us -> 176 us  [shards(): lax.all_to_all(snapshots.reshape(GROUPS, each, NFFT), 'freq', 0, 0, axis_...]
    all_to_all x1, blocking collectives: 33.5 us -> 44.9 us  [shards(): mine = jnp.sum(lax.all_to_all(mine, 'freq', 0, 0), 0)]
    ppermute x1, starting transfers between devices: 2.49 us -> 6.95 us  [shards(): other = lax.ppermute(other, 'space', [(s, s ^ 1) for s in range(GROUPS)])]
where the time goes in v5:
time: 299 us
  waiting for transfers between devices  177 us (59%)
  blocking collectives  76.4 us (26%)
  starting transfers between devices  36.4 us (12%)
  Pallas kernels  7.24 us (2%)
    all_to_all x1, waiting for transfers between devices, shards(): lax.all_to_all(snapshots.reshape(GROUPS, each, NFFT), 'freq', 0, 0, axis_...  176 us
    all_to_all x1, blocking collectives, shards(): mine = jnp.sum(lax.all_to_all(mine, 'freq', 0, 0), 0)  44.9 us
    all_to_all x1, starting transfers between devices, shards(): lax.all_to_all(snapshots.reshape(GROUPS, each, NFFT), 'freq', 0, 0, axis_...  29.4 us
    all_to_all x1, blocking collectives, shards(): lax.all_to_all(sums.astype(jnp.bfloat16), 'space', 0, 0, axis_index_group...  17.3 us
    all_to_all x1, blocking collectives, shards(): lax.all_to_all(jnp.broadcast_to(mine[None], (GROUPS,) + mine.shape), 'spa...  14.2 us
    ppermute x1, starting transfers between devices, shards(): other = lax.ppermute(other, 'space', [(s, s ^ 1) for s in range(GROUPS)])  6.95 us
  transfers between devices with their start and end apart: 2, of which 2 were waited for; matrix products, arithmetic and copies ran while one was open for 0% of the time, Pallas kernels for 0%

profile of v5, /device:TPU:1, one launch (start us, length us, event | category | flops | bytes accessed | tf_op | source)
XLA Modules:
  0.0 298.9 jit_solution(13111311626051318795)
XLA Ops:
  0.6 0.0 copy-start
  0.6 29.4 %all-to-all-start = ((bf16[32,128,256]{2,1,0:T(8,128)(2,1)}), bf16[32,128,256]{2,1,0:T(8,128)(2,1)S(1)}, u32[]{:S(2)}, u32[]{:S(2)}) async-start(bf16[32,128,256]{2,1,0:T(8,128)(2,1)} %bitcast.5), calls=%async_computation | async-start | bytes 4194304 | tf_op jit(solution)/shard_map/all_to_all | solution.py:203
  30.3 0.0 copy-done
  30.3 0.5 multiply_convert_fusion
  30.9 175.6 %all-to-all-done.raw_ref = bf16[32,128,256]{2,1,0:T(8,128)(2,1)S(1)} async-done(((bf16[32,128,256]{2,1,0:T(8,128)(2,1)}), bf16[32,128,256]{2,1,0:T(8,128)(2,1)S(1)}, u32[]{:S(2)}, u32[]{:S(2)}) %all-to-all-start) | async-done | bytes 2097184 | tf_op jit(solution)/shard_map/all_to_all | solution.py:203
  206.4 5.4 %gram.1 = (f32[16,128,128]{2,1,0:T(8,128)S(1)}, bf16[16,128,128]{2,1,0:T(8,128)(2,1)S(1)}) custom-call(s32[1]{0:T(128)} %bitcast.1.core_ref, f32[1]{0:T(128)} %bitcast.2.factor_ref, bf16[32,128,256]{2,1,0:T(8,128)(2,1)S(1)} %all-to-all-done.raw_ref, bf16[128,128]{1,0:T(8,128)(2,1)S(1)} %constant_dynamic-slice_fusion.tail_ref, ...), custom_call_target="tpu_custom_call" | custom-call | tf_op jit(solution)/shard_map/gram/pallas_call | solution.py:87
  211.8 0.0 copy-start.1
  211.8 7.0 %collective-permute-start = (bf16[16,128,128]{2,1,0:T(8,128)(2,1)S(1)}, bf16[16,128,128]{2,1,0:T(8,128)(2,1)S(1)}, u32[]{:S(2)}, u32[]{:S(2)}) collective-permute-start(bf16[16,128,128]{2,1,0:T(8,128)(2,1)S(1)} %get-tuple-element.5), channel_id=1, source_target_pairs={{0,32},{32,0},{64,96},{96,64},{128,160},{160,128},{192,224},{224,1... | collective-permute-start | bytes 1572872 | tf_op jit(solution)/shard_map/ppermute | solution.py:212
  218.8 1.5 collective-permute-done
  220.3 0.1 add_convert_fusion
  220.5 17.3 %all_to_all.20 = bf16[16,128,128]{2,1,0:T(8,128)(2,1)S(1)} all-to-all(bf16[16,128,128]{2,1,0:T(8,128)(2,1)S(1)} %add_convert_fusion), channel_id=1, replica_groups={{0,64,128,192,256,320,384,448,512,576,640,704,768,832,896,960},{32,96,1..., dimensions={0} | all-to-all | bytes 1048576 | tf_op jit(solution)/shard_map/all_to_all | solution.py:215
  237.7 0.0 copy-done.1
  237.7 0.2 multiply_reduce_fusion
  237.9 44.9 %all_to_all.21 = f32[32,4,128]{2,1,0:T(4,128)S(1)} all-to-all(f32[32,4,128]{2,1,0:T(4,128)S(1)} %bitcast.6), channel_id=1, replica_groups=mesh['space'=32,'freq'=32] {'freq'}, dimensions={0} | all-to-all | bytes 131072 | tf_op jit(solution)/shard_map/all_to_all | solution.py:223
  282.9 14.2 %all_to_all.22.sums_ref = f32[32,4,128]{2,1,0:T(4,128)S(1)} all-to-all(f32[32,4,128]{2,1,0:T(4,128)S(1)} %broadcast_in_dim.2), channel_id=1, replica_groups=mesh['space'=32,'freq'=32] {'space'}, dimensions={0} | all-to-all | bytes 131072 | tf_op jit(solution)/shard_map/all_to_all | solution.py:224
  297.1 1.9 power.1
  (6 shorter events, 0.2 us)
Async XLA Ops:
  0.6 29.6 %copy-start = (bf16[4096,128]{1,0:T(8,128)(2,1)S(1)}, bf16[4096,128]{1,0:T(8,128)(2,1)}, u32[]{:S(2)}) copy-start(bf16[4096,128]{1,0:T(8,128)(2,1)} %param.4) | copy-start | bytes 3145732
  0.6 205.8 %all-to-all-start = ((bf16[32,128,256]{2,1,0:T(8,128)(2,1)}), bf16[32,128,256]{2,1,0:T(8,128)(2,1)S(1)}, u32[]{:S(2)}, u32[]{:S(2)}) async-start(bf16[32,128,256]{2,1,0:T(8,128)(2,1)} %bitcast.5), calls=%async_computation | async-start | bytes 4194304 | tf_op jit(solution)/shard_map/all_to_all | solution.py:203
  211.8 25.9 %copy-start.1 = (f32[16]{0:T(128)S(1)}, f32[16]{0:T(128)}, u32[]{:S(2)}) copy-start(f32[16]{0:T(128)} %constant.92.clone) | copy-start | bytes 196
  211.8 8.5 %collective-permute-start = (bf16[16,128,128]{2,1,0:T(8,128)(2,1)S(1)}, bf16[16,128,128]{2,1,0:T(8,128)(2,1)S(1)}, u32[]{:S(2)}, u32[]{:S(2)}) collective-permute-start(bf16[16,128,128]{2,1,0:T(8,128)(2,1)S(1)} %get-tuple-element.5), channel_id=1, source_target_pairs={{0,32},{32,0},{64,96},{96,64},{128,160},{160,128},{192,224},{224,1... | collective-permute-start | bytes 1572872 | tf_op jit(solution)/shard_map/ppermute | solution.py:212
